TPU v7x, 512 devices: a whole 4x8x8 slice. The times are simulated.
512 devices in a mesh: dp: 32 (over x, y), tp: 16 (over z, core).
Axes of the slice: x: 4, y: 8, z: 8, core: 2. Of those that a mesh axis runs over, the one named last changes fastest.
Arguments:
- embeddings: bfloat16 [12288, 192, 256], P(('dp', 'tp')), may hold values from -6 to 6
- projection: bfloat16 [256, 16], replicated, may hold values from -0.375 to 0.375
- compress: bfloat16 [256, 4], replicated, may hold values from -0.375 to 0.375
- w_up: bfloat16 [4096, 4096], P(None, 'tp'), may hold values from -0.09375 to 0.09375
- w_down: bfloat16 [4096, 768], P('tp'), may hold values from -0.125 to 0.125
- output_norm_gain: float32 [1536], P('tp'), may hold values from 0.25 to 1.75
- out_grad: bfloat16 [12288, 1536], P('dp', 'tp'), may hold values from -6 to 6
Outputs:
- block_result: bfloat16 [12288, 1536], P('dp', 'tp')
- grad_down: float32 [4096, 768], P(('tp', 'dp'))
All inputs are finite; a program needn't handle non-finite values.
Results may differ from a plain program's by a relative error of at most 0.017.
Values may be sent and summed in bfloat16 or wider, within the bound.
No kernel may reach another device: no remote copies, remote signals or barrier semaphores. Data moves between devices by JAX's collectives and lax.ppermute only.
A program may use at most 64 MiB of HBM per device.

v0:
```python
import jax
import jax.numpy as jnp
from jax import lax
from jax.sharding import PartitionSpec as P

BF16, F16, F32 = (jnp.bfloat16, jnp.float16, jnp.float32)
NORMED_SCALE, LCB_SCALE, GG_SCALE = (512.0, 64.0, 4096.0)


def high_low(x):
    high = lax.reduce_precision(x, 8, 7)
    return (high.astype(BF16), (x - high).astype(BF16))


def on_device(embeddings, projection, compress, w_up, w_down, output_norm_gain, out_grad):
    samples, edim, fields = embeddings.shape
    tp = lax.axis_size("tp")
    dp = lax.axis_size("dp")
    me = lax.axis_index("tp")
    core = me % 2
    group_rows = samples * tp
    feat, fmw = (w_up.shape[0], w_down.shape[1])
    own = fmw // tp
    width = 2 * own
    pairs = jnp.einsum("sef,fk->sek", embeddings, projection, preferred_element_type=F32).astype(
        BF16
    )
    inter = jnp.einsum("sek,sef->skf", pairs, embeddings, preferred_element_type=F32).reshape(
        samples, -1
    )
    center = inter - jnp.mean(inter, axis=1, keepdims=True)
    spread = jnp.mean(center * center, axis=1, keepdims=True)
    normed = (center * (NORMED_SCALE / jnp.sqrt(spread + 1e-05))).astype(F16)
    lcb = jnp.einsum("sef,fj->sje", embeddings, compress, preferred_element_type=F32).reshape(
        samples, -1
    )
    gg = out_grad.T.astype(F32) * output_norm_gain[:, None]
    gg_packed = (
        (gg[:own] * GG_SCALE)
        .astype(F16)
        .reshape(3, 2, 8, group_rows)
        .transpose(0, 2, 1, 3)
        .reshape(samples, -1)
    )
    sent = jnp.concatenate([normed, (lcb * LCB_SCALE).astype(F16), gg_packed], axis=1)
    got = lax.all_gather(sent, "tp", axis=0, tiled=True)
    pre = jnp.dot(got[:, :feat].astype(BF16), w_up, preferred_element_type=F32)
    hidden = jax.nn.gelu(pre * (1.0 / NORMED_SCALE), approximate=True).astype(BF16)
    mlp = jnp.einsum("hc,sh->cs", w_down, hidden, preferred_element_type=F32)
    mlp = mlp.reshape(tp // 2, 2, own, group_rows)
    swap = [(i, i ^ 1) for i in range(tp)]
    theirs = lax.dynamic_index_in_dim(mlp, 1 - core, 1, keepdims=False).astype(BF16)
    mine = lax.dynamic_index_in_dim(mlp, core, 1, keepdims=False)
    chip_sum = (mine + lax.ppermute(theirs, "tp", swap).astype(F32)).astype(BF16)
    same_core = [list(range(c, tp, 2)) for c in range(2)]
    arrived = lax.all_to_all(chip_sum, "tp", 0, 0, tiled=True, axis_index_groups=same_core)
    mlp_own = arrived.astype(F32).sum(axis=0)
    lcb_own = lax.dynamic_slice_in_dim(got[:, feat : feat + fmw], me * own, own, 1)
    lcb_own = lcb_own.astype(F32).T * (1.0 / LCB_SCALE)
    mix = jnp.concatenate([mlp_own, lcb_own], axis=0)
    own_mean = jnp.mean(mix, axis=0)
    delta = mix - own_mean
    own_dev = jnp.sum(delta * delta, axis=0)
    own_g = jnp.sum(gg, axis=0)
    own_gd = jnp.sum(gg * delta, axis=0)
    stats = jnp.stack([own_mean, own_dev, own_g, own_gd])
    message = jnp.concatenate([delta[:own].astype(BF16), *high_low(stats)], axis=0)
    every = lax.all_gather(message, "tp", axis=0, tiled=False)
    numbers = every[:, own : own + 4].astype(F32) + every[:, own + 4 :].astype(F32)
    means, devs, gs, gds = (numbers[:, k] for k in range(4))
    full = width * tp
    mean = jnp.mean(means, axis=0)
    shift = means - mean
    var = (jnp.sum(devs, axis=0) + width * jnp.sum(shift * shift, axis=0)) / full
    rstd = 1.0 / jnp.sqrt(var + 1e-05)
    first = jnp.sum(gs, axis=0) / full
    second = jnp.sum(gds + shift * gs, axis=0) * rstd / full
    block = (delta + (own_mean - mean)) * rstd * output_norm_gain[:, None]
    block_result = block.astype(BF16).T
    gg_all = (
        got[:, feat + fmw :]
        .reshape(tp, 3, 8, 2, group_rows)
        .transpose(0, 1, 3, 2, 4)
        .reshape(tp, own, group_rows)
    )
    xhat = (every[:, :own].astype(F32) + shift[:, None]) * rstd
    dmix = ((gg_all.astype(F32) * (1.0 / GG_SCALE) - first - xhat * second) * rstd).astype(BF16)
    dmix = dmix.reshape(fmw, group_rows)
    grad = jnp.einsum("sh,cs->hc", hidden, dmix, preferred_element_type=F32).astype(BF16)
    parts = lax.all_to_all(grad.reshape(dp, -1, fmw), "dp", 0, 0, tiled=True)
    return (block_result, parts.astype(F32).sum(axis=0))


def solution(mesh):
    return jax.shard_map(
        on_device,
        mesh=mesh,
        in_specs=(
            P(("dp", "tp"), None, None),
            P(),
            P(),
            P(None, "tp"),
            P("tp", None),
            P("tp"),
            P("dp", "tp"),
        ),
        out_specs=(P("dp", "tp"), P(("tp", "dp"), None)),
        check_vma=False,
    )
```

profile of v0, /device:TPU:8, one launch (start us, length us, event | category | flops | bytes accessed | tf_op | source)
XLA Modules:
  0.0 120.3 jit_solution(396855091383316326)
XLA Ops:
  0.6 0.0 copy-start
  0.7 1.6 %copy-done = bf16[24,192,256]{2,1,0:T(8,128)(2,1)S(1)} copy-done((bf16[24,192,256]{2,1,0:T(8,128)(2,1)S(1)}, bf16[24,192,256]{2,1,0:T(8,128)(2,1)}, u32[]{:S(2)}) %copy-start) | copy-done | bytes 2359320
  2.3 0.0 copy-start.7
  2.3 0.0 copy-start.10
  2.3 0.0 copy-start.9
  2.3 1.4 %fusion.8 = f16[24,4,192]{2,1,0:T(4,128)(2,1)S(1)} fusion(bf16[24,192,256]{2,1,0:T(8,128)(2,1)S(1)} %copy-done, bf16[256,4]{0,1:T(4,128)(2,1)} %param.9), kind=kOutput, calls=%fused_computation.15 | convolution fusion | flops 9474048 | bytes 2398208 | tf_op jit(solution)/shard_map/sef,fj->sje/dot_general | solution.py:34
  3.7 0.1 convert_element_type.84
  3.9 0.0 copy-done.7
  3.9 0.0 copy-done.10
  3.9 0.1 fusion.19
  4.0 0.0 copy-done.9
  4.0 1.1 fusion.33
  5.1 0.4 multiply_reduce_fusion
  5.5 0.2 copy.52
  5.8 0.1 multiply_convert_fusion
  5.9 0.1 pad_maximum_fusion
  6.0 0.0 copy-start.11
  6.0 38.7 %all-gather.2 = f16[384,5632]{1,0:T(8,128)(2,1)S(1)} all-gather(f16[24,5632]{1,0:T(8,128)(2,1)S(1)} %pad_maximum_fusion), channel_id=1, replica_groups=mesh['dp'=32,'tp'=16] {'tp'}, dimensions={0}, use_global_device_ids=true | all-gather | bytes 4595712 | tf_op jit(solution)/shard_map/all_gather | solution.py:46
  44.7 0.0 copy-done.11
  44.7 0.0 copy-start.1
  44.7 0.0 copy-start.6
  44.7 1.0 fusion.17
  45.8 0.9 copy-done.1
  46.7 0.0 copy-start.2
  46.7 0.7 copy-done.2
  47.4 0.0 copy-done.6
  47.4 0.3 convolution_bitcast_fusion
  47.7 1.4 %copy.40 = f32[768,384]{1,0:T(8,128)} copy(f32[768,384]{0,1:T(8,128)S(1)} %convolution_bitcast_fusion) | data formatting | bytes 2359296 | tf_op jit(solution)/shard_map/hc,sh->cs/dot_general | solution.py:49
  49.1 1.1 fusion.18
  50.2 2.3 %collective-permute-start = (bf16[8,48,384]{2,1,0:T(8,128)(2,1)S(1)}, bf16[8,48,384]{2,1,0:T(8,128)(2,1)S(1)}, u32[]{:S(2)}, u32[]{:S(2)}) collective-permute-start(bf16[8,48,384]{2,1,0:T(8,128)(2,1)S(1)} %fusion.18), channel_id=1, source_target_pairs={{0,1},{1,0},{2,3},{3,2},{4,5},{5,4},{6,7},{7,6},{8,9},{9,8},{10,11... | collective-permute-start | bytes 884744 | tf_op jit(solution)/shard_map/ppermute | solution.py:54
  52.5 0.0 slice-start
  52.5 1.2 collective-permute-done
  53.7 1.9 %fusion.9 = bf16[8,48,384]{2,1,0:T(8,128)(2,1)} fusion(bf16[8,48,384]{2,1,0:T(8,128)(2,1)S(1)} %collective-permute-done, f32[8,2,48,384]{3,2,1,0:T(8,128)} %bitcast.76, s32[]{:T(128)S(6)} %select_n.18), kind=kLoop, calls=%fused_computation.21 | loop fusion | flops 442368 | bytes 1179652 | tf_op jit(solution)/shard_map/convert_element_type | solution.py:54
  55.5 4.1 %all-to-all-start = ((bf16[8,48,384]{2,1,0:T(8,128)(2,1)}), bf16[8,48,384]{2,1,0:T(8,128)(2,1)}, u32[]{:S(2)}, u32[]{:S(2)}) async-start(bf16[8,48,384]{2,1,0:T(8,128)(2,1)} %fusion.9), calls=%async_computation | async-start | bytes 589824 | tf_op jit(solution)/shard_map/all_to_all | solution.py:56
  59.6 0.0 slice-done
  59.6 0.1 constant_dynamic-slice_fusion
  59.8 0.7 copy.47
  60.5 1.2 convert_multiply_fusion
  61.7 1.6 %mul.195 = f32[16,3,8,2,384]{4,3,2,1,0:T(2,128)} reshape(f32[384,768]{1,0:T(8,128)S(1)} %convert_multiply_fusion) | data formatting | bytes 2359296 | tf_op jit(solution)/shard_map/mul | solution.py:87
  63.3 0.0 copy-start.8
  63.3 1.4 %copy.43 = f32[16,3,2,8,384]{4,3,2,1,0:T(8,128)S(1)} copy(f32[16,3,2,8,384]{4,2,3,1,0:T(2,128)} %bitcast.74) | data formatting | bytes 2359296 | tf_op jit(solution)/shard_map/mul | solution.py:87
  64.7 0.0 copy-done.8
  64.7 0.6 fusion.24
  65.3 7.7 %all-to-all-done = bf16[8,48,384]{2,1,0:T(8,128)(2,1)} async-done(((bf16[8,48,384]{2,1,0:T(8,128)(2,1)}), bf16[8,48,384]{2,1,0:T(8,128)(2,1)}, u32[]{:S(2)}, u32[]{:S(2)}) %all-to-all-start) | async-done | bytes 294944 | tf_op jit(solution)/shard_map/all_to_all | solution.py:56
  73.0 1.1 convert_reduce_fusion.1
  74.1 1.0 multiply_reduce_fusion.2
  75.1 0.0 copy-start.4
  75.2 16.6 %all-gather = bf16[896,384]{1,0:T(8,128)(2,1)S(1)} all-gather(bf16[56,384]{1,0:T(8,128)(2,1)S(1)} %pad_maximum_fusion.1), channel_id=2, replica_groups=mesh['dp'=32,'tp'=16] {'tp'}, dimensions={0}, use_global_device_ids=true | all-gather | bytes 731136 | tf_op jit(solution)/shard_map/all_gather | solution.py:68
  91.8 0.1 slice_reduce_fusion.1
  92.0 0.0 copy-done.4
  92.0 0.0 copy-start.3
  92.0 0.3 fusion.5
  92.3 0.0 copy-start.5
  92.3 0.6 copy-done.3
  92.9 1.1 fusion.1
  94.1 10.2 %all-to-all-start.1 = ((bf16[32,8,768]{2,1,0:T(8,128)(2,1)}), bf16[32,8,768]{2,1,0:T(8,128)(2,1)S(1)}, u32[]{:S(2)}, u32[]{:S(2)}) async-start(bf16[32,8,768]{2,1,0:T(8,128)(2,1)} %fusion.1), calls=%async_computation.1 | async-start | bytes 786432 | tf_op jit(solution)/shard_map/all_to_all | solution.py:90
  104.2 0.0 copy-done.5
  104.3 0.7 fusion.21
  105.0 14.7 %all-to-all-done.1 = bf16[32,8,768]{2,1,0:T(8,128)(2,1)S(1)} async-done(((bf16[32,8,768]{2,1,0:T(8,128)(2,1)}), bf16[32,8,768]{2,1,0:T(8,128)(2,1)S(1)}, u32[]{:S(2)}, u32[]{:S(2)}) %all-to-all-start.1) | async-done | bytes 393248 | tf_op jit(solution)/shard_map/all_to_all | solution.py:90
  119.7 0.7 convert_reduce_fusion
  (16 shorter events, 0.2 us)
Async XLA Ops:
  0.6 1.7 %copy-start = (bf16[24,192,256]{2,1,0:T(8,128)(2,1)S(1)}, bf16[24,192,256]{2,1,0:T(8,128)(2,1)}, u32[]{:S(2)}) copy-start(bf16[24,192,256]{2,1,0:T(8,128)(2,1)} %param.7) | copy-start | bytes 7077892
  2.3 1.6 %copy-start.7 = (bf16[384,96]{0,1:T(8,128)(2,1)S(1)}, bf16[384,96]{0,1:T(8,128)(2,1)}, u32[]{:S(2)}) copy-start(bf16[384,96]{0,1:T(8,128)(2,1)} %param.13) | copy-start | bytes 221188
  2.3 1.6 %copy-start.10 = (f32[96]{0:T(128)S(1)}, f32[96]{0:T(128)}, u32[]{:S(2)}) copy-start(f32[96]{0:T(128)} %param.12) | copy-start | bytes 1156
  2.3 1.7 %copy-start.9 = (bf16[256,16]{0,1:T(8,128)(2,1)S(1)}, bf16[256,16]{0,1:T(8,128)(2,1)}, u32[]{:S(2)}) copy-start(bf16[256,16]{0,1:T(8,128)(2,1)} %param.8) | copy-start | bytes 24580
  6.0 38.7 %copy-start.11 = (bf16[4096,256]{1,0:T(8,128)(2,1)S(1)}, bf16[4096,256]{1,0:T(8,128)(2,1)}, u32[]{:S(2)}) copy-start(bf16[4096,256]{1,0:T(8,128)(2,1)} %param.10) | copy-start | bytes 6291460
  44.7 2.0 %copy-start.1 = (f16[384,5632]{1,0:T(8,128)(2,1)}, f16[384,5632]{1,0:T(8,128)(2,1)S(1)}, u32[]{:S(2)}) copy-start(f16[384,5632]{1,0:T(8,128)(2,1)S(1)} %all-gather.2) | copy-start | bytes 12976132
  44.7 2.7 %copy-start.6 = (bf16[256,768]{1,0:T(8,128)(2,1)S(1)}, bf16[256,768]{1,0:T(8,128)(2,1)}, u32[]{:S(2)}) copy-start(bf16[256,768]{1,0:T(8,128)(2,1)} %param.11) | copy-start | bytes 1179652
  46.7 0.7 copy-start.2
  50.2 3.5 %collective-permute-start = (bf16[8,48,384]{2,1,0:T(8,128)(2,1)S(1)}, bf16[8,48,384]{2,1,0:T(8,128)(2,1)S(1)}, u32[]{:S(2)}, u32[]{:S(2)}) collective-permute-start(bf16[8,48,384]{2,1,0:T(8,128)(2,1)S(1)} %fusion.18), channel_id=1, source_target_pairs={{0,1},{1,0},{2,3},{3,2},{4,5},{5,4},{6,7},{7,6},{8,9},{9,8},{10,11... | collective-permute-start | bytes 884744 | tf_op jit(solution)/shard_map/ppermute | solution.py:54
  52.5 7.1 %slice-start = ((f16[384,5632]{1,0:T(8,128)(2,1)}), f16[384,768]{1,0:T(8,128)(2,1)S(1)}, s32[]{:S(2)}) async-start(f16[384,5632]{1,0:T(8,128)(2,1)} %copy-done.1), calls=%async_computation.2 | async-start | bytes 1179648 | tf_op jit(solution)/shard_map/slice | solution.py:58
  55.5 17.5 %all-to-all-start = ((bf16[8,48,384]{2,1,0:T(8,128)(2,1)}), bf16[8,48,384]{2,1,0:T(8,128)(2,1)}, u32[]{:S(2)}, u32[]{:S(2)}) async-start(bf16[8,48,384]{2,1,0:T(8,128)(2,1)} %fusion.9), calls=%async_computation | async-start | bytes 589824 | tf_op jit(solution)/shard_map/all_to_all | solution.py:56
  63.3 1.4 %copy-start.8 = (f16[384,48]{0,1:T(8,128)(2,1)S(1)}, f16[384,48]{0,1:T(8,128)(2,1)}, u32[]{:S(2)}) copy-start(f16[384,48]{0,1:T(8,128)(2,1)} %copy.47) | copy-start | bytes 110596
  75.1 16.9 %copy-start.4 = (f32[96,384]{1,0:T(8,128)}, f32[96,384]{1,0:T(8,128)S(1)}, u32[]{:S(2)}) copy-start(f32[96,384]{1,0:T(8,128)S(1)} %get-tuple-element.15) | copy-start | bytes 442372
  92.0 0.9 copy-start.3
  92.3 11.9 %copy-start.5 = (f32[96,384]{1,0:T(8,128)S(1)}, f32[96,384]{1,0:T(8,128)}, u32[]{:S(2)}) copy-start(f32[96,384]{1,0:T(8,128)} %copy-done.4) | copy-start | bytes 442372
  94.1 25.6 %all-to-all-start.1 = ((bf16[32,8,768]{2,1,0:T(8,128)(2,1)}), bf16[32,8,768]{2,1,0:T(8,128)(2,1)S(1)}, u32[]{:S(2)}, u32[]{:S(2)}) async-start(bf16[32,8,768]{2,1,0:T(8,128)(2,1)} %fusion.1), calls=%async_computation.1 | async-start | bytes 786432 | tf_op jit(solution)/shard_map/all_to_all | solution.py:90
where the time goes:
time: 121 us; the launch traced here: 120 us
  blocking collectives  55.3 us (46%)
  waiting for transfers between devices  23.5 us (19%)
  starting transfers between devices  16.5 us (14%)
  local copies, waits for them, and re-layouts  10.6 us (9%)
  other arithmetic  8.4 us (7%)
  matrix products  5.05 us (4%)
    all_gather x1, blocking collectives, on_device(): got = lax.all_gather(sent, 'tp', axis=0, tiled=True)  38.7 us
    all_gather x1, blocking collectives, on_device(): every = lax.all_gather(message, 'tp', axis=0, tiled=False)  16.6 us
    all_to_all x1, waiting for transfers between devices, on_device(): parts = lax.all_to_all(grad.reshape(dp, -1, fmw), 'dp', 0, 0, tiled=True)  14.7 us
    all_to_all x1, starting transfers between devices, on_device(): parts = lax.all_to_all(grad.reshape(dp, -1, fmw), 'dp', 0, 0, tiled=True)  10.2 us
    all_to_all x1, waiting for transfers between devices, on_device(): lax.all_to_all(chip_sum, 'tp', 0, 0, tiled=True, axis_index_groups=same_c...  7.68 us
    unnamed x26, local copies, waits for them, and re-layouts  4.87 us
    all_to_all x1, starting transfers between devices, on_device(): lax.all_to_all(chip_sum, 'tp', 0, 0, tiled=True, axis_index_groups=same_c...  4.06 us
    mul x2, local copies, waits for them, and re-layouts, on_device(): gg_all.astype(F32) * (1.0 / GG_SCALE) - first - xhat * second  2.98 us
  transfers between devices with their start and end apart: 3, of which 3 were waited for; matrix products, arithmetic and copies ran while one was open for 5% of the time, Pallas kernels for 0%

commit v1 on v0

--- a/solution.py
+++ b/solution.py
@@ -43,7 +43,8 @@
         .reshape(samples, -1)
     )
     sent = jnp.concatenate([normed, (lcb * LCB_SCALE).astype(F16), gg_packed], axis=1)
-    got = lax.all_gather(sent, "tp", axis=0, tiled=True)
+    outgoing = jnp.stack([sent] * lax.axis_size("tp"))
+    got = jnp.concatenate(lax.all_to_all(outgoing, "tp", 0, 0), axis=0)
     pre = jnp.dot(got[:, :feat].astype(BF16), w_up, preferred_element_type=F32)
     hidden = jax.nn.gelu(pre * (1.0 / NORMED_SCALE), approximate=True).astype(BF16)
     mlp = jnp.einsum("hc,sh->cs", w_down, hidden, preferred_element_type=F32)

time: 121 us -> 196 us (1.62)
  waiting for transfers between devices: 23.5 us -> 119 us
  blocking collectives: 55.3 us -> 16.6 us
  starting transfers between devices: 16.5 us -> 27.2 us
  local copies, waits for them, and re-layouts: 10.6 us -> 14.6 us
  matrix products: 5.05 us -> 7.62 us
    all_to_all x0 -> x1, waiting for transfers between devices: none -> 97.1 us  [on_device(): got = jnp.concatenate(lax.all_to_all(outgoing, 'tp', 0, 0), axis=0)]
    all_gather x1 -> x0, blocking collectives: 38.7 us -> none  [on_device(): got = lax.all_gather(sent, 'tp', axis=0, tiled=True)]
    all_to_all x0 -> x1, starting transfers between devices: none -> 10.5 us  [on_device(): got = jnp.concatenate(lax.all_to_all(outgoing, 'tp', 0, 0), axis=0)]
    dot_general x1, matrix products: 1.05 us -> 3.63 us  [on_device(): pre = jnp.dot(got[:, :feat].astype(BF16), w_up, preferred_element_type=F32)]
    another operation x0 -> x1, local copies, waits for them, and re-layouts: none -> 2.29 us  [on_device(): outgoing = jnp.stack([sent] * lax.axis_size('tp'))]
    unnamed x26 -> x22, local copies, waits for them, and re-layouts: 4.87 us -> 2.82 us
    slice x2 -> x1, local copies, waits for them, and re-layouts: 0.01 us -> 2.02 us  [on_device(): got[:, feat:feat + fmw]]
  transfers between devices with their start and end apart: 3 -> 4, of which waited for: 3 -> 3; matrix products, arithmetic and copies ran while one was open for 5% -> 5% of each run, Pallas kernels for 0% -> 0%
where the time goes in v1:
time: 196 us; the launch traced here: 195 us
  waiting for transfers between devices  119 us (61%)
  starting transfers between devices  27.2 us (14%)
  blocking collectives  16.6 us (8%)
  local copies, waits for them, and re-layouts  14.6 us (7%)
  other arithmetic  9.31 us (5%)
  matrix products  7.62 us (4%)
    all_to_all x1, waiting for transfers between devices, on_device(): got = jnp.concatenate(lax.all_to_all(outgoing, 'tp', 0, 0), axis=0)  97.1 us
    all_gather x1, blocking collectives, on_device(): every = lax.all_gather(message, 'tp', axis=0, tiled=False)  16.6 us
    all_to_all x1, waiting for transfers between devices, on_device(): parts = lax.all_to_all(grad.reshape(dp, -1, fmw), 'dp', 0, 0, tiled=True)  14.7 us
    all_to_all x1, starting transfers between devices, on_device(): got = jnp.concatenate(lax.all_to_all(outgoing, 'tp', 0, 0), axis=0)  10.5 us
    all_to_all x1, starting transfers between devices, on_device(): parts = lax.all_to_all(grad.reshape(dp, -1, fmw), 'dp', 0, 0, tiled=True)  10.2 us
    all_to_all x1, waiting for transfers between devices, on_device(): lax.all_to_all(chip_sum, 'tp', 0, 0, tiled=True, axis_index_groups=same_c...  6.76 us
    all_to_all x1, starting transfers between devices, on_device(): lax.all_to_all(chip_sum, 'tp', 0, 0, tiled=True, axis_index_groups=same_c...  4.69 us
  transfers between devices with their start and end apart: 4, of which 3 were waited for; matrix products, arithmetic and copies ran while one was open for 5% of the time, Pallas kernels for 0%

profile of v1, /device:TPU:8, one launch (start us, length us, event | category | flops | bytes accessed | tf_op | source)
XLA Modules:
  0.0 194.8 jit_solution(2700624138864377551)
XLA Ops:
  0.6 0.0 copy-start
  0.6 1.1 fusion.19
  1.8 0.6 copy-done
  2.4 0.0 copy-start.8
  2.4 1.4 fusion.8
  3.8 0.1 convert_element_type.84
  3.9 0.0 copy-done.8
  3.9 1.1 fusion.32
  5.0 0.2 copy.29
  5.3 0.4 multiply_reduce_fusion
  5.7 0.1 multiply_convert_fusion
  5.8 0.1 pad_maximum_fusion
  5.9 2.3 %stack.10 = f16[16,24,5632]{2,1,0:T(8,128)(2,1)} broadcast(f16[24,5632]{1,0:T(8,128)(2,1)S(1)} %pad_maximum_fusion), dimensions={1,2} | broadcast | bytes 4595712 | tf_op jit(solution)/shard_map/stack | solution.py:46
  8.2 10.5 %all-to-all-start = ((f16[16,24,5632]{2,1,0:T(8,128)(2,1)}), f16[16,24,5632]{2,1,0:T(8,128)(2,1)}, u32[]{:S(2)}, u32[]{:S(2)}) async-start(f16[16,24,5632]{2,1,0:T(8,128)(2,1)} %stack.10), calls=%async_computation | async-start | bytes 8650752 | tf_op jit(solution)/shard_map/all_to_all | solution.py:47
  18.7 97.1 %all-to-all-done = f16[16,24,5632]{2,1,0:T(8,128)(2,1)} async-done(((f16[16,24,5632]{2,1,0:T(8,128)(2,1)}), f16[16,24,5632]{2,1,0:T(8,128)(2,1)}, u32[]{:S(2)}, u32[]{:S(2)}) %all-to-all-start) | async-done | bytes 4325408 | tf_op jit(solution)/shard_map/all_to_all | solution.py:47
  115.8 0.0 copy-start.6
  115.8 3.6 %fusion.17 = bf16[384,256]{1,0:T(8,128)(2,1)S(1)} fusion(bf16[4096,256]{1,0:T(8,128)(2,1)} %param.10, f16[384,5632]{1,0:T(8,128)(2,1)} %bitcast.7), kind=kOutput, calls=%fused_computation.30 | convolution fusion | flops 807862272 | bytes 5439488 | tf_op jit(solution)/shard_map/dot_general | solution.py:48
  119.4 0.0 copy-start.2
  119.4 0.7 copy-done.2
  120.1 0.0 copy-done.6
  120.1 0.3 convolution_bitcast_fusion
  120.4 1.4 copy.19
  121.8 0.0 copy-start.1
  121.8 1.9 fusion.18
  123.7 1.9 collective-permute-start
  125.6 2.0 %slice.51 = f16[384,768]{1,0:T(8,128)(2,1)} slice(f16[384,5632]{1,0:T(8,128)(2,1)} %bitcast.7), slice={[0:384], [4096:4864]} | slice | bytes 1179648 | tf_op jit(solution)/shard_map/slice | solution.py:59
  127.6 0.0 collective-permute-done
  127.6 0.0 copy-done.1
  127.6 1.7 fusion.9
  129.4 4.7 %all-to-all-start.1 = ((bf16[8,48,384]{2,1,0:T(8,128)(2,1)}), bf16[8,48,384]{2,1,0:T(8,128)(2,1)}, u32[]{:S(2)}, u32[]{:S(2)}) async-start(bf16[8,48,384]{2,1,0:T(8,128)(2,1)} %fusion.9), calls=%async_computation.1 | async-start | bytes 589824 | tf_op jit(solution)/shard_map/all_to_all | solution.py:57
  134.1 1.0 constant_dynamic-slice_fusion
  135.1 0.7 copy.26
  135.9 1.2 convert_multiply_fusion
  137.0 1.6 mul.195
  138.7 0.0 copy-start.7
  138.7 0.0 copy-start.9
  138.7 1.4 copy.22
  140.0 0.0 copy-done.7
  140.0 0.6 fusion.24
  140.7 6.8 %all-to-all-done.1 = bf16[8,48,384]{2,1,0:T(8,128)(2,1)} async-done(((bf16[8,48,384]{2,1,0:T(8,128)(2,1)}), bf16[8,48,384]{2,1,0:T(8,128)(2,1)}, u32[]{:S(2)}, u32[]{:S(2)}) %all-to-all-start.1) | async-done | bytes 294944 | tf_op jit(solution)/shard_map/all_to_all | solution.py:57
  147.4 1.1 convert_reduce_fusion.1
  148.5 0.0 copy-done.9
  148.5 1.0 multiply_reduce_fusion.2
  149.5 0.0 copy-start.4
  149.6 16.6 %all-gather = bf16[896,384]{1,0:T(8,128)(2,1)S(1)} all-gather(bf16[56,384]{1,0:T(8,128)(2,1)S(1)} %pad_maximum_fusion.1), channel_id=2, replica_groups=mesh['dp'=32,'tp'=16] {'tp'}, dimensions={0}, use_global_device_ids=true | all-gather | bytes 731136 | tf_op jit(solution)/shard_map/all_gather | solution.py:69
  166.2 0.1 slice_reduce_fusion.1
  166.4 0.0 copy-done.4
  166.4 0.0 copy-start.3
  166.4 0.3 fusion.5
  166.8 0.0 copy-start.5
  166.8 0.6 copy-done.3
  167.4 1.1 fusion.1
  168.5 10.2 %all-to-all-start.2 = ((bf16[32,8,768]{2,1,0:T(8,128)(2,1)}), bf16[32,8,768]{2,1,0:T(8,128)(2,1)S(1)}, u32[]{:S(2)}, u32[]{:S(2)}) async-start(bf16[32,8,768]{2,1,0:T(8,128)(2,1)} %fusion.1), calls=%async_computation.2 | async-start | bytes 786432 | tf_op jit(solution)/shard_map/all_to_all | solution.py:91
  178.7 0.0 copy-done.5
  178.7 0.7 fusion.21
  179.4 14.7 %all-to-all-done.2 = bf16[32,8,768]{2,1,0:T(8,128)(2,1)S(1)} async-done(((bf16[32,8,768]{2,1,0:T(8,128)(2,1)}), bf16[32,8,768]{2,1,0:T(8,128)(2,1)S(1)}, u32[]{:S(2)}, u32[]{:S(2)}) %all-to-all-start.2) | async-done | bytes 393248 | tf_op jit(solution)/shard_map/all_to_all | solution.py:91
  194.1 0.7 convert_reduce_fusion
  (16 shorter events, 0.2 us)
Async XLA Ops:
  0.6 1.7 copy-start
  2.4 1.5 copy-start.8
  8.2 107.6 %all-to-all-start = ((f16[16,24,5632]{2,1,0:T(8,128)(2,1)}), f16[16,24,5632]{2,1,0:T(8,128)(2,1)}, u32[]{:S(2)}, u32[]{:S(2)}) async-start(f16[16,24,5632]{2,1,0:T(8,128)(2,1)} %stack.10), calls=%async_computation | async-start | bytes 8650752 | tf_op jit(solution)/shard_map/all_to_all | solution.py:47
  115.8 4.3 %copy-start.6 = (bf16[256,768]{1,0:T(8,128)(2,1)S(1)}, bf16[256,768]{1,0:T(8,128)(2,1)}, u32[]{:S(2)}) copy-start(bf16[256,768]{1,0:T(8,128)(2,1)} %param.11) | copy-start | bytes 1179652
  119.4 0.7 copy-start.2
  121.8 5.9 %copy-start.1 = (f32[768,384]{1,0:T(8,128)S(1)}, f32[768,384]{1,0:T(8,128)}, u32[]{:S(2)}) copy-start(f32[768,384]{1,0:T(8,128)} %copy.19) | copy-start | bytes 3538948
  123.7 4.0 %collective-permute-start = (bf16[8,48,384]{2,1,0:T(8,128)(2,1)}, bf16[8,48,384]{2,1,0:T(8,128)(2,1)}, u32[]{:S(2)}, u32[]{:S(2)}) collective-permute-start(bf16[8,48,384]{2,1,0:T(8,128)(2,1)} %fusion.18), channel_id=1, source_target_pairs={{0,1},{1,0},{2,3},{3,2},{4,5},{5,4},{6,7},{7,6},{8,9},{9,8},{10,11... | collective-permute-start | bytes 884744 | tf_op jit(solution)/shard_map/ppermute | solution.py:55
  129.4 18.1 %all-to-all-start.1 = ((bf16[8,48,384]{2,1,0:T(8,128)(2,1)}), bf16[8,48,384]{2,1,0:T(8,128)(2,1)}, u32[]{:S(2)}, u32[]{:S(2)}) async-start(bf16[8,48,384]{2,1,0:T(8,128)(2,1)} %fusion.9), calls=%async_computation.1 | async-start | bytes 589824 | tf_op jit(solution)/shard_map/all_to_all | solution.py:57
  138.7 1.4 copy-start.7
  138.7 9.9 %copy-start.9 = (f32[96]{0:T(128)S(1)}, f32[96]{0:T(128)}, u32[]{:S(2)}) copy-start(f32[96]{0:T(128)} %param.12) | copy-start | bytes 1156
  149.5 16.9 %copy-start.4 = (f32[96,384]{1,0:T(8,128)}, f32[96,384]{1,0:T(8,128)S(1)}, u32[]{:S(2)}) copy-start(f32[96,384]{1,0:T(8,128)S(1)} %get-tuple-element.15) | copy-start | bytes 442372
  166.4 0.9 copy-start.3
  166.8 11.9 %copy-start.5 = (f32[96,384]{1,0:T(8,128)S(1)}, f32[96,384]{1,0:T(8,128)}, u32[]{:S(2)}) copy-start(f32[96,384]{1,0:T(8,128)} %copy-done.4) | copy-start | bytes 442372
  168.5 25.6 %all-to-all-start.2 = ((bf16[32,8,768]{2,1,0:T(8,128)(2,1)}), bf16[32,8,768]{2,1,0:T(8,128)(2,1)S(1)}, u32[]{:S(2)}, u32[]{:S(2)}) async-start(bf16[32,8,768]{2,1,0:T(8,128)(2,1)} %fusion.1), calls=%async_computation.2 | async-start | bytes 786432 | tf_op jit(solution)/shard_map/all_to_all | solution.py:91
